TPU v7x, 256 devices: a whole 4x4x8 slice. The times are simulated.
256 devices in a mesh: band: 8 (over x, core), dom: 32 (over z, y).
Axes of the slice: x: 4, y: 4, z: 8, core: 2. Of those that a mesh axis runs over, the one named last changes fastest.
Arguments:
- orbitals: bfloat16 [256, 192, 48, 64], P('band', 'dom'), may hold values from -1.796875 to 1.796875
- potential: float32 [192, 48, 64], P('dom'), may hold values from -2 to 1
- projectors: float32 [2048, 128], P('dom'), may hold values from -1.5 to 1.5
- coupling: float32 [1024], P('dom'), may hold values from 0.5 to 2
- slot_block: int32 [2048], P('dom'), may hold values from 0 to 143
- slot_projector: int32 [2048], P('dom'), may hold values from 0 to 1023, as said below
- slot_count: int32 [32], P('dom'), may hold values from 16 to 64, as said below
- locked: bfloat16 [2048, 192, 3072], P(None, 'dom', 'band'), may hold values from -0.0078125 to 0.0078125
Outputs:
- orthogonal: bfloat16 [256, 192, 3072], P(None, 'dom', 'band')
- margins: float32 [2048, 256], P(('band', 'dom'))
Inputs may be any that keep to these rules, and one draw needn't show every extreme that they name: `slot_projector`: projector p belongs to domain p // 32; a slot of domain d names a projector of domain d - 1, d or d + 1, cyclically; slot 0 of every domain names one of domain d - 1 and slot 1 one of domain d + 1. The used slots of a domain are its first slot_count slots; some domain uses all and some uses 64 // 4.
All inputs are finite; a program needn't handle non-finite values.
Results may differ from a plain program's by a relative error of at most 0.0039.
The roundings to bfloat16 on the way count: a program that leaves them out, or rounds other values in their place, can miss the bound.
Values may be sent and summed in bfloat16 or wider, within the bound.
No kernel may reach another device: no remote copies, remote signals or barrier semaphores. Data moves between devices by JAX's collectives and lax.ppermute only.
A program may use at most 320 MiB of HBM per device.

v0:
```python
import jax
import jax.numpy as jnp
from jax import lax
from jax.sharding import PartitionSpec as P

BS = 128
PROJ_DOM = 32
COEFFS = (
    -5369.0 / 1800.0,
    12.0 / 7.0,
    -15.0 / 56.0,
    10.0 / 189.0,
    -1.0 / 112.0,
    2.0 / 825.0,
    -1.0 / 5544.0,
)


def with_halo(shard, sides, width):
    for axis, dim in sides:
        size, length = (lax.axis_size(axis), shard.shape[dim])
        up = [(i, (i + 1) % size) for i in range(size)]
        down = [(j, i) for i, j in up]
        last = lax.slice_in_dim(shard, length - width, length, axis=dim)
        initial = lax.slice_in_dim(shard, 0, width, axis=dim)
        before = lax.ppermute(last, axis, up)
        after = lax.ppermute(initial, axis, down)
        shard = jnp.concatenate([before, shard, after], axis=dim)
    return shard


def laplacian(orbital, extended):
    planes_x = orbital.shape[1]
    depth_z = orbital.shape[2]
    laplace = 3.0 * COEFFS[0] * orbital
    padded = jnp.pad(orbital, ((0, 0), (0, 0), (6, 6), (0, 0)))
    for offset in range(1, 7):
        weight = COEFFS[offset]
        laplace = laplace + weight * (
            extended[:, 6 + offset : 6 + offset + planes_x]
            + extended[:, 6 - offset : 6 - offset + planes_x]
        )
        laplace = laplace + weight * (jnp.roll(orbital, offset, 3) + jnp.roll(orbital, -offset, 3))
        laplace = laplace + weight * (
            padded[:, :, 6 + offset : 6 + offset + depth_z]
            + padded[:, :, 6 - offset : 6 - offset + depth_z]
        )
    return laplace


def per_device(
    orbitals, potential, projectors, coupling, slot_block, slot_projector, slot_count, locked
):
    orbital = orbitals.astype(jnp.float32)
    extended = with_halo(orbitals, (("dom", 1),), 6).astype(jnp.float32)
    laplace = laplacian(orbital, extended)
    band_rows, planes_x, depth_z, width_y = orbital.shape
    blocks_count = planes_x * depth_z * width_y // BS
    flat = orbital.reshape(band_rows, blocks_count, BS)
    blocks = flat[:, slot_block]
    slots = slot_block.shape[0]
    active = (jnp.arange(slots, dtype=jnp.int32) < slot_count[0]).astype(jnp.float32)
    inner_part = jnp.sum(blocks * projectors[None], axis=2) * active[None]
    domains = lax.axis_size("dom")
    here = lax.axis_index("dom")
    owner = slot_projector // PROJ_DOM
    local_id = slot_projector % PROJ_DOM
    relative = (owner - here + domains) % domains
    column = jnp.where(
        relative == 0,
        PROJ_DOM + local_id,
        jnp.where(relative == 1, 2 * PROJ_DOM + local_id, local_id),
    )
    onehot = (column[:, None] == jnp.arange(3 * PROJ_DOM, dtype=jnp.int32)[None, :]).astype(
        jnp.float32
    )
    partial_value = jnp.dot(inner_part, onehot, precision=lax.Precision.HIGHEST)
    outgoing = jnp.concatenate(
        [partial_value[:, :PROJ_DOM], partial_value[:, 2 * PROJ_DOM :]], axis=1
    )
    arrived = with_halo(outgoing, (("dom", 1),), PROJ_DOM)
    owned = (
        partial_value[:, PROJ_DOM : 2 * PROJ_DOM] + arrived[:, :PROJ_DOM] + arrived[:, -PROJ_DOM:]
    )
    table_local = owned * coupling[None]
    table = with_halo(table_local, (("dom", 1),), PROJ_DOM)
    slot_value = jnp.dot(table, onehot.T, precision=lax.Precision.HIGHEST) * active[None]
    contribution = slot_value[:, :, None] * projectors[None]
    nonlocal_term = jnp.zeros_like(flat).at[:, slot_block].add(contribution).reshape(orbital.shape)
    hamilton = -0.5 * laplace + potential[None] * orbital + nonlocal_term
    numerator, denominator = lax.psum(
        (jnp.sum(orbital * hamilton, axis=(1, 2, 3)), jnp.sum(orbital * orbital, axis=(1, 2, 3))),
        "dom",
    )
    energy = numerator / denominator
    residual = (hamilton - energy[:, None, None, None] * orbital).astype(jnp.bfloat16)
    residual = residual.reshape(band_rows, planes_x, depth_z * width_y)
    moved = lax.all_to_all(residual, "band", split_axis=2, concat_axis=0, tiled=True)
    all_bands = moved.shape[0]
    locked_flat = locked.reshape(locked.shape[0], -1)
    residual_flat = moved.reshape(all_bands, -1)
    contract_cells = (((1,), (1,)), ((), ()))
    share_rows = locked.shape[0] // lax.axis_size(("band", "dom"))
    summed = lax.psum(
        lax.dot_general(
            locked_flat, residual_flat, contract_cells, preferred_element_type=jnp.float32
        ),
        ("band", "dom"),
    )
    margins = lax.dynamic_slice_in_dim(
        summed, lax.axis_index(("band", "dom")) * share_rows, share_rows, 0
    )
    coeffs = summed.astype(jnp.bfloat16)
    correction = lax.dot_general(
        coeffs, locked_flat, (((0,), (0,)), ((), ())), preferred_element_type=jnp.float32
    )
    orthogonal = (
        (residual_flat.astype(jnp.float32) - correction).astype(jnp.bfloat16).reshape(moved.shape)
    )
    return (orthogonal, margins)


def solution(mesh):
    in_specs = (
        P("band", "dom", None, None),
        P("dom", None, None),
        P("dom", None),
        P("dom"),
        P("dom"),
        P("dom"),
        P("dom"),
        P(None, "dom", "band"),
    )
    out_specs = (P(None, "dom", "band"), P(("band", "dom"), None))
    return jax.shard_map(
        per_device, mesh=mesh, in_specs=in_specs, out_specs=out_specs, check_vma=False
    )
```

profile of v0, /device:TPU:2, one launch (start us, length us, event | category | flops | bytes accessed | tf_op | source)
XLA Modules:
  0.0 610.1 jit_solution(6926809845291708726)
XLA Ops:
  7.2 0.0 copy-start.4
  7.2 1.7 collective-permute-start
  8.8 6.8 %collective-permute-start.1 = (bf16[32,6,48,64]{3,2,1,0:T(8,128)(2,1)}, bf16[32,6,48,64]{3,2,1,0:T(8,128)(2,1)}, u32[]{:S(2)}, u32[]{:S(2)}) collective-permute-start(bf16[32,6,48,64]{3,2,1,0:T(8,128)(2,1)} %param.8), channel_id=1, source_target_pairs={{1,0},{2,1},{3,2},{4,3},{5,4},{6,5},{7,6},{8,7},{9,8},{10,9},{11,1... | collective-permute-start | bytes 3538952 | tf_op jit(solution)/shard_map/ppermute | solution.py:27
  15.7 4.4 reshape.34
  20.0 0.0 copy-done.4
  20.1 4.0 copy.30
  24.7 0.0 copy-done.5
  24.7 2.3 gather_fusion
  27.0 0.0 copy-done.2
  27.0 0.3 multiply_reduce_fusion
  27.4 0.3 fusion.50
  27.7 0.1 fusion.77
  27.7 0.0 collective-permute-start.2
  27.8 5.8 collective-permute-start.3
  33.5 4.6 fusion.65
  38.1 4.7 fusion.66
  42.8 4.7 fusion.67
  47.5 4.6 fusion.68
  52.1 4.6 fusion.69
  56.8 4.6 fusion.70
  61.3 4.7 fusion.71
  66.0 4.6 fusion.72
  70.6 4.6 fusion.73
  75.2 4.7 fusion.74
  79.9 4.6 fusion.75
  84.5 0.0 collective-permute-done.2
  84.5 0.0 collective-permute-done.3
  84.5 0.0 copy-done.3
  84.5 0.1 fusion.53
  84.6 0.0 collective-permute-start.4
  84.7 5.5 collective-permute-start.5
  90.2 4.7 fusion.76
  94.9 2.7 convert_element_type.28
  97.6 0.0 collective-permute-done.4
  97.6 0.0 collective-permute-done.5
  97.6 0.2 convolution_multiply_fusion
  97.7 0.1 copy.31
  97.9 0.3 multiply_bitcast_fusion
  98.2 1.7 broadcast_in_dim.4
  99.9 8.0 %scatter_fusion = f32[32,144,128]{2,0,1:T(8,128)} fusion(f32[32,144,128]{2,0,1:T(8,128)} %broadcast_in_dim.4, s32[64]{0:T(128)S(1)} %compare_select_fusion, f32[64,32,128]{2,1,0:T(8,128)S(1)} %multiply_bitcast_fusion), kind=kCustom, calls=%fused_computation.1 | custom fusion | flops 262144 | bytes 3145984 | tf_op jit(solution)/shard_map/scatter-add | solution.py:89
  108.0 4.5 copy.32
  112.4 4.5 reshape.35
  117.0 0.0 collective-permute-done
  117.0 0.0 collective-permute-done.1
  117.0 8.1 %maximum_convert_fusion = f32[32,18,48,64]{3,2,1,0:T(8,128)} fusion(bf16[32,6,48,64]{3,2,1,0:T(8,128)(2,1)} %collective-permute-done.1, bf16[32,6,48,64]{3,2,1,0:T(8,128)(2,1)S(1)} %copy-done, bf16[32,6,48,64]{3,2,1,0:T(8,128)(2,1)} %collective-permute-done), kind=kLoop, calls=%fused_computation.14 | loop fusion | flops 5308416 | bytes 10616832 | tf_op jit(solution)/shard_map/convert_element_type | solution.py:55
  125.1 75.7 %fusion.21 = (f32[32]{0:T(128)S(1)}, f32[32]{0:T(128)S(1)}, f32[32,6,48,64]{3,2,1,0:T(8,128)}) fusion(bf16[32,6,48,64]{3,2,1,0:T(8,128)(2,1)S(1)} %copy-done, f32[32,6,48,64]{3,2,1,0:T(8,128)} %reshape.35, f32[6,48,64]{2,1,0:T(8,128)S(1)} %copy-done.1, f32[32,6,48,6]{3,2,1,0:T(8,128)} %get-tuple-element.36, f32[32,6,48,58]{3,2,1,0:T(8,128)} %get-tuple-element.38, ...), kind=kLoop, calls=%fused_computation.41 | loop fusion | flops 44826560 | bytes 64954624 | tf_op jit(solution)/shard_map/reduce_sum | solution.py:92
  200.8 69.9 %all-reduce.1 = (f32[32]{0:T(128)S(1)}, f32[32]{0:T(128)S(1)}) all-reduce(f32[32]{0:T(128)S(1)} %get-tuple-element.11, f32[32]{0:T(128)S(1)} %get-tuple-element.10), channel_id=1, replica_groups=mesh['band'=8,'dom'=32] {'dom'}, use_global_device_ids=true, to_apply=%region_3.4 | all-reduce | flops 64 | bytes 512 | tf_op jit(solution)/shard_map/psum | solution.py:91
  270.7 4.6 fusion.23
  275.2 7.8 %copy.45 = bf16[32,6,48,64]{0,1,3,2:T(8,128)(2,1)} copy(bf16[32,6,48,64]{3,2,1,0:T(8,128)(2,1)} %fusion.23) | data formatting | bytes 2359296 | tf_op jit(solution)/shard_map/reshape | solution.py:97
  283.0 8.6 %reshape.59 = bf16[8,2,36864]{2,1,0:T(2,128)(2,1)} reshape(bf16[3072,6,32]{2,1,0:T(8,128)(2,1)} %bitcast.23) | data formatting | bytes 2359296
  291.6 4.8 all-to-all-start
  296.5 12.5 %copy.37 = bf16[2048,6,384]{0,2,1:T(8,128)(2,1)} copy(bf16[2048,6,384]{2,0,1:T(8,128)(2,1)} %param.15) | data formatting | bytes 18874368 | tf_op args[7]
  309.0 3.4 all-to-all-done
  312.4 6.2 %reshape.60 = bf16[3072,6,32]{2,1,0:T(8,128)(2,1)} reshape(bf16[8,2,36864]{2,1,0:T(2,128)(2,1)S(1)} %all-to-all-done) | data formatting | bytes 2359296
  318.5 6.5 %copy.36 = bf16[8,32,6,384]{3,2,1,0:T(8,128)(2,1)S(1)} copy(bf16[8,32,6,384]{1,2,3,0:T(8,128)(2,1)} %bitcast.24) | data formatting | bytes 2359296 | tf_op jit(solution)/shard_map/all_to_all | solution.py:98
  325.1 0.2 copy.46
  325.2 7.7 %convolution_bitcast_fusion = f32[2048,256]{0,1:T(8,128)} fusion(bf16[256,2304]{1,0:T(8,128)(2,1)S(1)} %bitcast.29, bf16[2048,2304]{0,1:T(8,128)(2,1)} %bitcast.25), kind=kOutput, calls=%fused_computation.82 | convolution fusion | flops 2415919104 | bytes 12713984 | tf_op jit(solution)/shard_map/dot_general | solution.py:105
  333.0 0.0 all-reduce.4.cloned.1.call-update
  333.0 259.3 %all-reduce.4.cloned.1.call-done = f32[2048,256]{0,1:T(8,128)} async-done(((f32[2048,256]{0,1:T(8,128)}), f32[2048,256]{0,1:T(8,128)}) %all-reduce.4.cloned.1.call-update) | async-done | bytes 2097168 | tf_op jit(solution)/shard_map/psum | solution.py:104
  592.3 7.0 %fusion.48 = bf16[256,2304]{1,0:T(8,128)(2,1)S(1)} fusion(bf16[2048,2304]{0,1:T(8,128)(2,1)} %bitcast.26, bf16[256,2304]{1,0:T(8,128)(2,1)S(1)} %bitcast.30, f32[2048,256]{0,1:T(8,128)} %all-reduce.4.cloned.1.call-done), kind=kOutput, calls=%fused_computation.81 | convolution fusion | flops 2418212864 | bytes 13893632 | tf_op jit(solution)/shard_map/dot_general | solution.py:114
  599.3 0.6 copy.38
  599.9 1.4 copy.39
  601.4 1.0 constant_dynamic-slice_fusion
  602.4 0.7 copy.40
  (13 shorter events, 0.1 us)
Async XLA Ops:
  7.2 12.9 %copy-start.4 = (s32[64]{0:T(128)S(1)}, s32[64]{0:T(128)}, u32[]{:S(2)}) copy-start(s32[64]{0:T(128)} %param.12) | copy-start | bytes 772
  7.2 109.8 %collective-permute-start = (bf16[32,6,48,64]{3,2,1,0:T(8,128)(2,1)}, bf16[32,6,48,64]{3,2,1,0:T(8,128)(2,1)}, u32[]{:S(2)}, u32[]{:S(2)}) collective-permute-start(bf16[32,6,48,64]{3,2,1,0:T(8,128)(2,1)} %param.8), channel_id=1, source_target_pairs={{0,1},{1,2},{2,3},{3,4},{4,5},{5,6},{6,7},{7,8},{8,9},{9,10},{10,1... | collective-permute-start | bytes 3538952 | tf_op jit(solution)/shard_map/ppermute | solution.py:26
  8.8 108.2 %collective-permute-start.1 = (bf16[32,6,48,64]{3,2,1,0:T(8,128)(2,1)}, bf16[32,6,48,64]{3,2,1,0:T(8,128)(2,1)}, u32[]{:S(2)}, u32[]{:S(2)}) collective-permute-start(bf16[32,6,48,64]{3,2,1,0:T(8,128)(2,1)} %param.8), channel_id=1, source_target_pairs={{1,0},{2,1},{3,2},{4,3},{5,4},{6,5},{7,6},{8,7},{9,8},{10,9},{11,1... | collective-permute-start | bytes 3538952 | tf_op jit(solution)/shard_map/ppermute | solution.py:27
  15.7 9.1 %copy-start.5 = (s32[64]{0:T(128)S(1)}, s32[64]{0:T(128)}, u32[]{:S(2)}) copy-start(s32[64]{0:T(128)} %param.13) | copy-start | bytes 772
  15.7 11.4 %copy-start.2 = (f32[64,128]{1,0:T(8,128)S(1)}, f32[64,128]{1,0:T(8,128)}, u32[]{:S(2)}) copy-start(f32[64,128]{1,0:T(8,128)} %param.10) | copy-start | bytes 98308
  20.0 13.5 %copy-start = (bf16[32,6,48,64]{3,2,1,0:T(8,128)(2,1)S(1)}, bf16[32,6,48,64]{3,2,1,0:T(8,128)(2,1)}, u32[]{:S(2)}) copy-start(bf16[32,6,48,64]{3,2,1,0:T(8,128)(2,1)} %param.8) | copy-start | bytes 3538948
  27.7 56.8 %collective-permute-start.2 = (f32[32,32]{1,0:T(8,128)S(1)}, f32[32,32]{1,0:T(8,128)S(1)}, u32[]{:S(2)}, u32[]{:S(2)}) collective-permute-start(f32[32,32]{1,0:T(8,128)S(1)} %get-tuple-element.39), channel_id=1, source_target_pairs={{0,1},{1,2},{2,3},{3,4},{4,5},{5,6},{6,7},{7,8},{8,9},{9,10},{10,1... | collective-permute-start | bytes 12296 | tf_op jit(solution)/shard_map/ppermute | solution.py:26
  27.8 56.8 %collective-permute-start.3 = (f32[32,32]{1,0:T(8,128)S(1)}, f32[32,32]{1,0:T(8,128)S(1)}, u32[]{:S(2)}, u32[]{:S(2)}) collective-permute-start(f32[32,32]{1,0:T(8,128)S(1)} %get-tuple-element.40), channel_id=1, source_target_pairs={{1,0},{2,1},{3,2},{4,3},{5,4},{6,5},{7,6},{8,7},{9,8},{10,9},{11,1... | collective-permute-start | bytes 12296 | tf_op jit(solution)/shard_map/ppermute | solution.py:27
  79.9 4.7 copy-start.3
  84.6 12.9 %collective-permute-start.4 = (f32[32,32]{1,0:T(8,128)S(1)}, f32[32,32]{1,0:T(8,128)S(1)}, u32[]{:S(2)}, u32[]{:S(2)}) collective-permute-start(f32[32,32]{1,0:T(8,128)S(1)} %fusion.53), channel_id=1, source_target_pairs={{0,1},{1,2},{2,3},{3,4},{4,5},{5,6},{6,7},{7,8},{8,9},{9,10},{10,1... | collective-permute-start | bytes 12296 | tf_op jit(solution)/shard_map/ppermute | solution.py:26
  84.7 12.9 %collective-permute-start.5 = (f32[32,32]{1,0:T(8,128)S(1)}, f32[32,32]{1,0:T(8,128)S(1)}, u32[]{:S(2)}, u32[]{:S(2)}) collective-permute-start(f32[32,32]{1,0:T(8,128)S(1)} %fusion.53), channel_id=1, source_target_pairs={{1,0},{2,1},{3,2},{4,3},{5,4},{6,5},{7,6},{8,7},{9,8},{10,9},{11,1... | collective-permute-start | bytes 12296 | tf_op jit(solution)/shard_map/ppermute | solution.py:27
  117.0 8.1 %copy-start.1 = (f32[6,48,64]{2,1,0:T(8,128)S(1)}, f32[6,48,64]{2,1,0:T(8,128)}, u32[]{:S(2)}) copy-start(f32[6,48,64]{2,1,0:T(8,128)} %param.9) | copy-start | bytes 221188
  291.6 20.7 %all-to-all-start = ((bf16[8,2,36864]{2,1,0:T(2,128)(2,1)}), bf16[8,2,36864]{2,1,0:T(2,128)(2,1)S(1)}, u32[]{:S(2)}, u32[]{:S(2)}) async-start(bf16[8,2,36864]{2,1,0:T(2,128)(2,1)} %reshape.59), calls=%async_computation | async-start | bytes 2359296 | tf_op jit(solution)/shard_map/all_to_all | solution.py:98
  296.5 295.9 %all-reduce.4.cloned.1.call-start = ((), (), s32[]{:S(2)}) async-start(), calls=%async_computation.1 | async-start | bytes 4194304 | tf_op jit(solution)/shard_map/psum | solution.py:104
Sparse Core Ops, SparseCore 0:
  333.1 259.1 all-reduce.3
where the time goes:
time: 616 us; the launch traced here: 610 us
  waiting for transfers between devices  263 us (43%)
  local copies, waits for them, and re-layouts  123 us (20%)
  other arithmetic  99.9 us (16%)
  blocking collectives  69.9 us (11%)
  starting transfers between devices  24.7 us (4%)
  matrix products  15.2 us (2%)
  between operations  15.1 us (2%)
    psum x1, waiting for transfers between devices, per_device(): lax.psum(lax.dot_general(locked_flat, residual_flat, contract_cells, pref...  259 us
    reduce_sum x1, other arithmetic, per_device(): jnp.sum(orbital * orbital, axis=(1, 2, 3))  75.7 us
    psum x1, blocking collectives, per_device(): lax.psum((jnp.sum(orbital * hamilton, axis=(1, 2, 3)), jnp.sum(orbital *...  69.9 us
    slice x12, local copies, waits for them, and re-layouts, laplacian(): jnp.roll(orbital, offset, 3) + jnp.roll(orbital, -offset, 3)  55.6 us
    unnamed x18, local copies, waits for them, and re-layouts  29.6 us
    ppermute x3, starting transfers between devices, with_halo(): after = lax.ppermute(initial, axis, down)  18.1 us
  transfers between devices with their start and end apart: 8, of which 2 were waited for; matrix products, arithmetic and copies ran while one was open for 17% of the time, Pallas kernels for 0%

commit v1 on v0

--- a/solution.py
+++ b/solution.py
@@ -2,6 +2,7 @@
 import jax.numpy as jnp
 from jax import lax
 from jax.sharding import PartitionSpec as P
+from jax.lax import psum
 
 BS = 128
 PROJ_DOM = 32
@@ -14,6 +15,12 @@
     2.0 / 825.0,
     -1.0 / 5544.0,
 )
+
+
+def terms_balance(slab_in):
+    for j0 in ("band", "dom"):
+        slab_in = psum(slab_in, j0)
+    return slab_in
 
 
 def with_halo(shard, sides, width):
@@ -101,11 +108,10 @@
     residual_flat = moved.reshape(all_bands, -1)
     contract_cells = (((1,), (1,)), ((), ()))
     share_rows = locked.shape[0] // lax.axis_size(("band", "dom"))
-    summed = lax.psum(
+    summed = terms_balance(
         lax.dot_general(
             locked_flat, residual_flat, contract_cells, preferred_element_type=jnp.float32
-        ),
-        ("band", "dom"),
+        )
     )
     margins = lax.dynamic_slice_in_dim(
         summed, lax.axis_index(("band", "dom")) * share_rows, share_rows, 0

time: 616 us -> 582 us (0.945)
  waiting for transfers between devices: 263 us -> 229 us
    psum x1 -> x2, waiting for transfers between devices: 259 us -> 226 us  [terms_balance(): slab_in = psum(slab_in, j0)]
  transfers between devices with their start and end apart: 8 -> 9, of which waited for: 2 -> 3; matrix products, arithmetic and copies ran while one was open for 17% -> 18% of each run, Pallas kernels for 0% -> 0%
where the time goes in v1:
time: 582 us; the launch traced here: 577 us
  waiting for transfers between devices  229 us (39%)
  local copies, waits for them, and re-layouts  123 us (21%)
  other arithmetic  99.9 us (17%)
  blocking collectives  69.9 us (12%)
  starting transfers between devices  24.7 us (4%)
  matrix products  15.2 us (3%)
  between operations  15.1 us (3%)
    psum x2, waiting for transfers between devices, terms_balance(): slab_in = psum(slab_in, j0)  226 us
    reduce_sum x1, other arithmetic, per_device(): jnp.sum(orbital * orbital, axis=(1, 2, 3))  75.7 us
    psum x1, blocking collectives, per_device(): lax.psum((jnp.sum(orbital * hamilton, axis=(1, 2, 3)), jnp.sum(orbital *...  69.9 us
    slice x12, local copies, waits for them, and re-layouts, laplacian(): jnp.roll(orbital, offset, 3) + jnp.roll(orbital, -offset, 3)  55.6 us
    unnamed x18, local copies, waits for them, and re-layouts  29.6 us
    ppermute x3, starting transfers between devices, with_halo(): after = lax.ppermute(initial, axis, down)  18.1 us
  transfers between devices with their start and end apart: 9, of which 3 were waited for; matrix products, arithmetic and copies ran while one was open for 18% of the time, Pallas kernels for 0%

profile of v1, /device:TPU:2, one launch (start us, length us, event | category | flops | bytes accessed | tf_op | source)
XLA Modules:
  0.0 576.9 jit_solution(3505558557735273261)
XLA Ops:
  7.2 1.7 collective-permute-start
  8.8 6.8 %collective-permute-start.1 = (bf16[32,6,48,64]{3,2,1,0:T(8,128)(2,1)}, bf16[32,6,48,64]{3,2,1,0:T(8,128)(2,1)}, u32[]{:S(2)}, u32[]{:S(2)}) collective-permute-start(bf16[32,6,48,64]{3,2,1,0:T(8,128)(2,1)} %param.8), channel_id=1, source_target_pairs={{1,0},{2,1},{3,2},{4,3},{5,4},{6,5},{7,6},{8,7},{9,8},{10,9},{11,1... | collective-permute-start | bytes 3538952 | tf_op jit(solution)/shard_map/ppermute | solution.py:34
  15.7 4.4 reshape.34
  20.1 4.0 copy.30
  24.7 2.3 gather_fusion
  27.0 0.0 copy-done.2
  27.0 0.3 multiply_reduce_fusion
  27.4 0.3 fusion.50
  27.7 0.1 fusion.77
  27.7 0.0 collective-permute-start.2
  27.8 5.8 %collective-permute-start.3 = (f32[32,32]{1,0:T(8,128)S(1)}, f32[32,32]{1,0:T(8,128)S(1)}, u32[]{:S(2)}, u32[]{:S(2)}) collective-permute-start(f32[32,32]{1,0:T(8,128)S(1)} %get-tuple-element.40), channel_id=1, source_target_pairs={{1,0},{2,1},{3,2},{4,3},{5,4},{6,5},{7,6},{8,7},{9,8},{10,9},{11,1... | collective-permute-start | bytes 12296 | tf_op jit(solution)/shard_map/ppermute | solution.py:34
  33.5 4.6 fusion.65
  38.1 4.7 fusion.66
  42.8 4.7 fusion.67
  47.5 4.6 fusion.68
  52.1 4.6 fusion.69
  56.8 4.6 fusion.70
  61.3 4.7 fusion.71
  66.0 4.6 fusion.72
  70.6 4.6 fusion.73
  75.2 4.7 fusion.74
  79.9 4.6 fusion.75
  84.5 0.0 collective-permute-done.2
  84.5 0.0 collective-permute-done.3
  84.5 0.0 copy-done.3
  84.5 0.1 fusion.53
  84.6 0.0 collective-permute-start.4
  84.7 5.5 collective-permute-start.5
  90.2 4.7 fusion.76
  94.9 2.7 convert_element_type.28
  97.6 0.0 collective-permute-done.4
  97.6 0.0 collective-permute-done.5
  97.6 0.2 convolution_multiply_fusion
  97.7 0.1 copy.31
  97.9 0.3 multiply_bitcast_fusion
  98.2 1.7 broadcast_in_dim.4
  99.9 8.0 %scatter_fusion = f32[32,144,128]{2,0,1:T(8,128)} fusion(f32[32,144,128]{2,0,1:T(8,128)} %broadcast_in_dim.4, s32[64]{0:T(128)S(1)} %compare_select_fusion, f32[64,32,128]{2,1,0:T(8,128)S(1)} %multiply_bitcast_fusion), kind=kCustom, calls=%fused_computation.1 | custom fusion | flops 262144 | bytes 3145984 | tf_op jit(solution)/shard_map/scatter-add | solution.py:96
  108.0 4.5 copy.32
  112.4 4.5 reshape.35
  117.0 0.0 collective-permute-done
  117.0 0.0 collective-permute-done.1
  117.0 8.1 %maximum_convert_fusion = f32[32,18,48,64]{3,2,1,0:T(8,128)} fusion(bf16[32,6,48,64]{3,2,1,0:T(8,128)(2,1)} %collective-permute-done.1, bf16[32,6,48,64]{3,2,1,0:T(8,128)(2,1)S(1)} %copy-done, bf16[32,6,48,64]{3,2,1,0:T(8,128)(2,1)} %collective-permute-done), kind=kLoop, calls=%fused_computation.14 | loop fusion | flops 5308416 | bytes 10616832 | tf_op jit(solution)/shard_map/convert_element_type | solution.py:62
  125.1 75.7 %fusion.21 = (f32[32]{0:T(128)S(1)}, f32[32]{0:T(128)S(1)}, f32[32,6,48,64]{3,2,1,0:T(8,128)}) fusion(bf16[32,6,48,64]{3,2,1,0:T(8,128)(2,1)S(1)} %copy-done, f32[32,6,48,64]{3,2,1,0:T(8,128)} %reshape.35, f32[6,48,64]{2,1,0:T(8,128)S(1)} %copy-done.1, f32[32,6,48,6]{3,2,1,0:T(8,128)} %get-tuple-element.36, f32[32,6,48,58]{3,2,1,0:T(8,128)} %get-tuple-element.38, ...), kind=kLoop, calls=%fused_computation.41 | loop fusion | flops 44826560 | bytes 64954624 | tf_op jit(solution)/shard_map/reduce_sum | solution.py:99
  200.8 69.9 %all-reduce.1 = (f32[32]{0:T(128)S(1)}, f32[32]{0:T(128)S(1)}) all-reduce(f32[32]{0:T(128)S(1)} %get-tuple-element.11, f32[32]{0:T(128)S(1)} %get-tuple-element.10), channel_id=1, replica_groups=mesh['band'=8,'dom'=32] {'dom'}, use_global_device_ids=true, to_apply=%region_3.4 | all-reduce | flops 64 | bytes 512 | tf_op jit(solution)/shard_map/psum | solution.py:98
  270.7 4.6 fusion.23
  275.2 7.8 %copy.45 = bf16[32,6,48,64]{0,1,3,2:T(8,128)(2,1)} copy(bf16[32,6,48,64]{3,2,1,0:T(8,128)(2,1)} %fusion.23) | data formatting | bytes 2359296 | tf_op jit(solution)/shard_map/reshape | solution.py:104
  283.0 8.6 %reshape.59 = bf16[8,2,36864]{2,1,0:T(2,128)(2,1)} reshape(bf16[3072,6,32]{2,1,0:T(8,128)(2,1)} %bitcast.23) | data formatting | bytes 2359296
  291.6 4.8 all-to-all-start
  296.5 12.5 %copy.37 = bf16[2048,6,384]{0,2,1:T(8,128)(2,1)} copy(bf16[2048,6,384]{2,0,1:T(8,128)(2,1)} %param.15) | data formatting | bytes 18874368 | tf_op args[7]
  309.0 3.4 all-to-all-done
  312.4 6.2 %reshape.60 = bf16[3072,6,32]{2,1,0:T(8,128)(2,1)} reshape(bf16[8,2,36864]{2,1,0:T(2,128)(2,1)S(1)} %all-to-all-done) | data formatting | bytes 2359296
  318.5 6.5 %copy.36 = bf16[8,32,6,384]{3,2,1,0:T(8,128)(2,1)S(1)} copy(bf16[8,32,6,384]{1,2,3,0:T(8,128)(2,1)} %bitcast.24) | data formatting | bytes 2359296 | tf_op jit(solution)/shard_map/all_to_all | solution.py:105
  325.1 0.2 copy.46
  325.2 7.7 %convolution_bitcast_fusion = f32[2048,256]{0,1:T(8,128)} fusion(bf16[256,2304]{1,0:T(8,128)(2,1)S(1)} %bitcast.29, bf16[2048,2304]{0,1:T(8,128)(2,1)} %bitcast.25), kind=kOutput, calls=%fused_computation.82 | convolution fusion | flops 2415919104 | bytes 12713984 | tf_op jit(solution)/shard_map/dot_general | solution.py:112
  333.0 0.0 all-reduce.5.cloned.1.call-update
  333.0 0.0 all-reduce.7.cloned.1.call-start
  333.1 66.2 %all-reduce.5.cloned.1.call-done = f32[2048,256]{0,1:T(8,128)} async-done(((f32[2048,256]{0,1:T(8,128)}), f32[2048,256]{0,1:T(8,128)}) %all-reduce.5.cloned.1.call-update) | async-done | bytes 2097168 | tf_op jit(solution)/shard_map/psum | solution.py:22
  399.3 0.0 all-reduce.7.cloned.1.call-update
  399.3 159.8 %all-reduce.7.cloned.1.call-done = f32[2048,256]{0,1:T(8,128)} async-done(((f32[2048,256]{0,1:T(8,128)}), f32[2048,256]{0,1:T(8,128)}) %all-reduce.7.cloned.1.call-update) | async-done | bytes 2097168 | tf_op jit(solution)/shard_map/psum | solution.py:22
  559.1 7.0 %fusion.48 = bf16[256,2304]{1,0:T(8,128)(2,1)S(1)} fusion(bf16[2048,2304]{0,1:T(8,128)(2,1)} %bitcast.26, bf16[256,2304]{1,0:T(8,128)(2,1)S(1)} %bitcast.30, f32[2048,256]{0,1:T(8,128)} %all-reduce.7.cloned.1.call-done), kind=kOutput, calls=%fused_computation.81 | convolution fusion | flops 2418212864 | bytes 13893632 | tf_op jit(solution)/shard_map/dot_general | solution.py:120
  566.1 0.6 copy.38
  566.7 1.4 copy.39
  568.1 1.0 constant_dynamic-slice_fusion
  569.1 0.7 copy.40
  (16 shorter events, 0.1 us)
Async XLA Ops:
  7.2 12.9 %copy-start.4 = (s32[64]{0:T(128)S(1)}, s32[64]{0:T(128)}, u32[]{:S(2)}) copy-start(s32[64]{0:T(128)} %param.12) | copy-start | bytes 772
  7.2 109.8 %collective-permute-start = (bf16[32,6,48,64]{3,2,1,0:T(8,128)(2,1)}, bf16[32,6,48,64]{3,2,1,0:T(8,128)(2,1)}, u32[]{:S(2)}, u32[]{:S(2)}) collective-permute-start(bf16[32,6,48,64]{3,2,1,0:T(8,128)(2,1)} %param.8), channel_id=1, source_target_pairs={{0,1},{1,2},{2,3},{3,4},{4,5},{5,6},{6,7},{7,8},{8,9},{9,10},{10,1... | collective-permute-start | bytes 3538952 | tf_op jit(solution)/shard_map/ppermute | solution.py:33
  8.8 108.2 %collective-permute-start.1 = (bf16[32,6,48,64]{3,2,1,0:T(8,128)(2,1)}, bf16[32,6,48,64]{3,2,1,0:T(8,128)(2,1)}, u32[]{:S(2)}, u32[]{:S(2)}) collective-permute-start(bf16[32,6,48,64]{3,2,1,0:T(8,128)(2,1)} %param.8), channel_id=1, source_target_pairs={{1,0},{2,1},{3,2},{4,3},{5,4},{6,5},{7,6},{8,7},{9,8},{10,9},{11,1... | collective-permute-start | bytes 3538952 | tf_op jit(solution)/shard_map/ppermute | solution.py:34
  15.7 9.1 %copy-start.5 = (s32[64]{0:T(128)S(1)}, s32[64]{0:T(128)}, u32[]{:S(2)}) copy-start(s32[64]{0:T(128)} %param.13) | copy-start | bytes 772
  15.7 11.4 %copy-start.2 = (f32[64,128]{1,0:T(8,128)S(1)}, f32[64,128]{1,0:T(8,128)}, u32[]{:S(2)}) copy-start(f32[64,128]{1,0:T(8,128)} %param.10) | copy-start | bytes 98308
  20.0 13.5 %copy-start = (bf16[32,6,48,64]{3,2,1,0:T(8,128)(2,1)S(1)}, bf16[32,6,48,64]{3,2,1,0:T(8,128)(2,1)}, u32[]{:S(2)}) copy-start(bf16[32,6,48,64]{3,2,1,0:T(8,128)(2,1)} %param.8) | copy-start | bytes 3538948
  27.7 56.8 %collective-permute-start.2 = (f32[32,32]{1,0:T(8,128)S(1)}, f32[32,32]{1,0:T(8,128)S(1)}, u32[]{:S(2)}, u32[]{:S(2)}) collective-permute-start(f32[32,32]{1,0:T(8,128)S(1)} %get-tuple-element.39), channel_id=1, source_target_pairs={{0,1},{1,2},{2,3},{3,4},{4,5},{5,6},{6,7},{7,8},{8,9},{9,10},{10,1... | collective-permute-start | bytes 12296 | tf_op jit(solution)/shard_map/ppermute | solution.py:33
  27.8 56.8 %collective-permute-start.3 = (f32[32,32]{1,0:T(8,128)S(1)}, f32[32,32]{1,0:T(8,128)S(1)}, u32[]{:S(2)}, u32[]{:S(2)}) collective-permute-start(f32[32,32]{1,0:T(8,128)S(1)} %get-tuple-element.40), channel_id=1, source_target_pairs={{1,0},{2,1},{3,2},{4,3},{5,4},{6,5},{7,6},{8,7},{9,8},{10,9},{11,1... | collective-permute-start | bytes 12296 | tf_op jit(solution)/shard_map/ppermute | solution.py:34
  79.9 4.7 copy-start.3
  84.6 12.9 %collective-permute-start.4 = (f32[32,32]{1,0:T(8,128)S(1)}, f32[32,32]{1,0:T(8,128)S(1)}, u32[]{:S(2)}, u32[]{:S(2)}) collective-permute-start(f32[32,32]{1,0:T(8,128)S(1)} %fusion.53), channel_id=1, source_target_pairs={{0,1},{1,2},{2,3},{3,4},{4,5},{5,6},{6,7},{7,8},{8,9},{9,10},{10,1... | collective-permute-start | bytes 12296 | tf_op jit(solution)/shard_map/ppermute | solution.py:33
  84.7 12.9 %collective-permute-start.5 = (f32[32,32]{1,0:T(8,128)S(1)}, f32[32,32]{1,0:T(8,128)S(1)}, u32[]{:S(2)}, u32[]{:S(2)}) collective-permute-start(f32[32,32]{1,0:T(8,128)S(1)} %fusion.53), channel_id=1, source_target_pairs={{1,0},{2,1},{3,2},{4,3},{5,4},{6,5},{7,6},{8,7},{9,8},{10,9},{11,1... | collective-permute-start | bytes 12296 | tf_op jit(solution)/shard_map/ppermute | solution.py:34
  117.0 8.1 %copy-start.1 = (f32[6,48,64]{2,1,0:T(8,128)S(1)}, f32[6,48,64]{2,1,0:T(8,128)}, u32[]{:S(2)}) copy-start(f32[6,48,64]{2,1,0:T(8,128)} %param.9) | copy-start | bytes 221188
  291.6 20.7 %all-to-all-start = ((bf16[8,2,36864]{2,1,0:T(2,128)(2,1)}), bf16[8,2,36864]{2,1,0:T(2,128)(2,1)S(1)}, u32[]{:S(2)}, u32[]{:S(2)}) async-start(bf16[8,2,36864]{2,1,0:T(2,128)(2,1)} %reshape.59), calls=%async_computation | async-start | bytes 2359296 | tf_op jit(solution)/shard_map/all_to_all | solution.py:105
  296.5 102.8 %all-reduce.5.cloned.1.call-start = ((), (), s32[]{:S(2)}) async-start(), calls=%async_computation.1 | async-start | bytes 4194304 | tf_op jit(solution)/shard_map/psum | solution.py:22
  333.0 226.1 %all-reduce.7.cloned.1.call-start = ((), (), s32[]{:S(2)}) async-start(), calls=%async_computation.2 | async-start | bytes 4194304 | tf_op jit(solution)/shard_map/psum | solution.py:22
Sparse Core Ops, SparseCore 0:
  333.1 66.1 all-reduce.4
  402.8 156.2 all-reduce.6
